TPU v7x, 32 devices: a whole 2x2x4 slice. The times are simulated.
32 devices in a mesh: outer: 8 (over y, x, core), inner: 4 (over z).
Axes of the slice: x: 2, y: 2, z: 4, core: 2. Of those that a mesh axis runs over, the one named last changes fastest.
Arguments:
- group_latents: bfloat16 [4096, 1024], P(('outer', 'inner')), may hold values from -6 to 6
- slot_ids: int32 [8, 4], P('outer', 'inner'), may hold values from 0 to 3, each once within a row
- slot_embed: bfloat16 [4, 1024], replicated, may hold values from -6 to 6
- merge_latents: bfloat16 [128, 2048], replicated, may hold values from -6 to 6
- query_weight: bfloat16 [2048, 2048], P(None, 'inner'), may hold values from -0.125 to 0.125
- key_weight: bfloat16 [1024, 2048], P(None, 'inner'), may hold values from -0.1875 to 0.1875
- value_weight: bfloat16 [1024, 2048], P(None, 'inner'), may hold values from -0.1875 to 0.1875
- output_weight: bfloat16 [2048, 2048], P('inner'), may hold values from -0.125 to 0.125
- global_latents: bfloat16 [1024, 2048], P(('outer', 'inner')), may hold values from -6 to 6
- decode_query: bfloat16 [2048, 2048], P(None, 'inner'), may hold values from -0.125 to 0.125
- decode_key: bfloat16 [2048, 2048], P(None, 'inner'), may hold values from -0.125 to 0.125
- decode_value: bfloat16 [2048, 2048], P(None, 'inner'), may hold values from -0.125 to 0.125
- decode_output: bfloat16 [2048, 2048], P('inner'), may hold values from -0.125 to 0.125
Outputs:
- decoded: bfloat16 [1024, 2048], P(('outer', 'inner'))
Inputs may be any that keep to these rules, and one draw needn't show every extreme that they name: `slot_ids`: each row holds every slot once.
All inputs are finite; a program needn't handle non-finite values.
Results may differ from a plain program's by a relative error of at most 0.014.
Values may be sent and summed in bfloat16 or wider, within the bound.
A program may use at most 64 MiB of HBM per device.

v0:
```python
import jax
import jax.numpy as jnp
from jax import lax
from jax.sharding import PartitionSpec as P

HEAD = 128


def attend(query_rows, key_rows, value_rows):
    length = query_rows.shape[0]
    head_count = query_rows.shape[1] // HEAD
    queries = query_rows.reshape(length, head_count, HEAD)
    keys_in = key_rows.reshape(key_rows.shape[0], head_count, HEAD)
    values_in = value_rows.reshape(value_rows.shape[0], head_count, HEAD)
    scores = jnp.einsum(
        "qhd,khd->hqk", queries, keys_in, preferred_element_type=jnp.float32
    ) * HEAD ** (-0.5)
    weights = jax.nn.softmax(scores, axis=-1).astype(jnp.bfloat16)
    mixed = jnp.einsum("hqk,khd->qhd", weights, values_in, preferred_element_type=jnp.float32)
    return mixed.reshape(length, head_count * HEAD).astype(jnp.bfloat16)


def local(
    group_latents,
    slot_ids,
    slot_embed,
    merge_latents,
    query_weight,
    key_weight,
    value_weight,
    output_weight,
    global_latents,
    decode_query,
    decode_key,
    decode_value,
    decode_output,
):
    columns = query_weight.shape[1]
    selector = (jnp.arange(slot_embed.shape[0], dtype=jnp.int32) == slot_ids[0, 0]).astype(
        jnp.bfloat16
    )
    slot_vector = jnp.dot(selector[None, :], slot_embed, preferred_element_type=jnp.float32)
    keyed = (group_latents.astype(jnp.float32) + slot_vector).astype(jnp.bfloat16)
    pair_two = jnp.concatenate([key_weight, value_weight], axis=1)
    keys_values = jnp.dot(
        lax.all_gather(keyed, "inner", axis=0, tiled=True),
        pair_two,
        preferred_element_type=jnp.float32,
    ).astype(jnp.bfloat16)
    query_two = jnp.dot(merge_latents, query_weight, preferred_element_type=jnp.float32).astype(
        jnp.bfloat16
    )
    mixed_two = attend(query_two, keys_values[:, :columns], keys_values[:, columns:])
    partial_value = jnp.dot(mixed_two, output_weight, preferred_element_type=jnp.float32)
    level_two = merge_latents.astype(jnp.float32) + lax.psum(
        partial_value.astype(jnp.bfloat16), "inner"
    ).astype(jnp.float32)
    normed = (
        level_two * lax.rsqrt(jnp.mean(level_two * level_two, axis=-1, keepdims=True) + 1e-06)
    ).astype(jnp.bfloat16)
    query_five = jnp.dot(normed, decode_query, preferred_element_type=jnp.float32).astype(
        jnp.bfloat16
    )
    pair_five = jnp.concatenate([decode_key, decode_value], axis=1)
    outer_block = lax.all_gather(global_latents, "inner", axis=0, tiled=True)
    global_pairs = lax.all_gather(
        jnp.dot(outer_block, pair_five, preferred_element_type=jnp.float32).astype(jnp.bfloat16),
        "outer",
        axis=0,
        tiled=True,
    )
    mixed_five = attend(query_five, global_pairs[:, :columns], global_pairs[:, columns:])
    own_rows = merge_latents.shape[0] // lax.axis_size("inner")
    summed = lax.psum_scatter(
        jnp.dot(mixed_five, decode_output, preferred_element_type=jnp.float32).astype(jnp.bfloat16),
        "inner",
        scatter_dimension=0,
        tiled=True,
    ).astype(jnp.float32)
    own_part = lax.dynamic_slice_in_dim(level_two, lax.axis_index("inner") * own_rows, own_rows, 0)
    return (own_part + summed).astype(jnp.bfloat16)


def solution(mesh):
    return jax.shard_map(
        local,
        mesh=mesh,
        in_specs=(
            P(("outer", "inner"), None),
            P("outer", "inner"),
            P(),
            P(),
            P(None, "inner"),
            P(None, "inner"),
            P(None, "inner"),
            P("inner", None),
            P(("outer", "inner"), None),
            P(None, "inner"),
            P(None, "inner"),
            P(None, "inner"),
            P("inner", None),
        ),
        out_specs=P(("outer", "inner"), None),
        check_vma=False,
    )
```

profile of v0, /device:TPU:0, one launch (start us, length us, event | category | flops | bytes accessed | tf_op | source)
XLA Modules:
  0.0 141.9 jit_solution(14467380582404468062)
XLA Ops:
  8.2 0.9 fusion.41
  9.1 1.7 %add_convert_fusion = bf16[128,1024]{1,0:T(8,128)(2,1)} fusion(bf16[128,1024]{1,0:T(8,128)(2,1)} %param.13, f32[1024]{0:T(1024)S(1)} %bitcast.67), kind=kLoop, calls=%fused_computation.37 | loop fusion | flops 393216 | bytes 528384 | tf_op jit(solution)/shard_map/convert_element_type | solution.py:43
  10.9 2.2 %fusion.22 = bf16[16,4,8,128]{3,2,1,0:T(8,128)(2,1)S(1)} fusion(bf16[128,2048]{1,0:T(8,128)(2,1)} %param.16, bf16[2048,512]{1,0:T(8,128)(2,1)} %param.17), kind=kOutput, calls=%fused_computation.26 | convolution fusion | flops 268500992 | bytes 2752512 | tf_op jit(solution)/shard_map/dot_general | solution.py:50
  13.1 28.5 %all-gather.3.cloned.1.call-done = bf16[512,1024]{1,0:T(8,128)(2,1)} async-done(((bf16[128,1024]{1,0:T(8,128)(2,1)}), bf16[512,1024]{1,0:T(8,128)(2,1)}) %all-gather.3.cloned.1.call-update) | async-done | bytes 1048592 | tf_op jit(solution)/shard_map/all_gather | solution.py:46
  41.6 2.8 %fusion.11 = bf16[512,1024]{1,0:T(8,128)(2,1)S(1)} fusion(bf16[512,1024]{1,0:T(8,128)(2,1)} %all-gather.3.cloned.1.call-done, bf16[1024,512]{1,0:T(8,128)(2,1)S(1)} %copy-done.5, bf16[1024,512]{1,0:T(8,128)(2,1)} %param.18), kind=kOutput, calls=%fused_computation.16 | convolution fusion | flops 1078460416 | bytes 4194304 | tf_op jit(solution)/shard_map/dot_general | solution.py:45
  44.4 0.1 slice_bitcast_fusion
  44.5 0.5 fusion.52
  45.0 1.3 convolution_multiply_fusion
  46.3 0.2 copy.20
  46.5 2.6 %convolution_convert_fusion.3 = bf16[4,128,128]{2,1,0:T(8,128)(2,1)S(1)} fusion(bf16[512,4,128]{0,2,1:T(8,128)(2,1)S(1)} %bitcast.64, f32[4,128]{1,0:T(4,128)S(1)} %fusion.52, f32[4,128,512]{2,1,0:T(8,128)} %convolution_multiply_fusion), kind=kOutput, calls=%fused_computation.23 | convolution fusion | flops 67961856 | bytes 1705984 | tf_op jit(solution)/shard_map/hqk,khd->qhd/dot_general | solution.py:19
  49.2 1.3 convolution_convert_fusion.1
  50.5 0.0 all-gather.5.cloned.1.call-start
  50.5 19.1 %all_gather.10 = bf16[128,2048]{1,0:T(8,128)(2,1)S(1)} all-gather(bf16[32,2048]{1,0:T(8,128)(2,1)S(1)} %copy-done.4), channel_id=1, replica_groups=mesh['outer'=8,'inner'=4] {'inner'}, dimensions={0}, use_global_device_ids=true | all-gather | bytes 655360 | tf_op jit(solution)/shard_map/all_gather | solution.py:65
  69.6 4.3 %fusion.19 = bf16[128,1024]{0,1:T(8,128)(2,1)} fusion(bf16[128,2048]{1,0:T(8,128)(2,1)S(1)} %all_gather.10, bf16[2048,512]{1,0:T(8,128)(2,1)} %param.24, bf16[2048,512]{1,0:T(8,128)(2,1)} %param.23), kind=kOutput, calls=%fused_computation.21 | convolution fusion | flops 545390592 | bytes 4980736 | tf_op jit(solution)/shard_map/dot_general | solution.py:67
  74.0 18.3 %all-reduce.2.cloned.1.call-done = bf16[128,2048]{1,0:T(8,128)(2,1)} async-done(((bf16[128,2048]{1,0:T(8,128)(2,1)}), bf16[128,2048]{1,0:T(8,128)(2,1)}) %all-reduce.2.cloned.1.call-update) | async-done | bytes 524304 | tf_op jit(solution)/shard_map/psum | solution.py:55
  92.3 2.5 %convert_add_fusion = (f32[128,2048]{1,0:T(8,128)}, f32[128]{0:T(128)S(1)}) fusion(bf16[128,2048]{1,0:T(8,128)(2,1)} %all-reduce.2.cloned.1.call-done, bf16[128,2048]{1,0:T(8,128)(2,1)S(1)} %copy-done.1), kind=kLoop, calls=%fused_computation.31 | loop fusion | flops 1310592 | bytes 2097664 | tf_op jit(solution)/shard_map/add | solution.py:55
  94.8 1.5 %fusion.23 = bf16[16,4,8,128]{3,2,1,0:T(8,128)(2,1)S(1)} fusion(bf16[2048,512]{1,0:T(8,128)(2,1)S(1)} %copy-done.2, f32[128]{0:T(128)S(1)} %add_rsqrt_fusion, bf16[128,2048]{1,0:T(8,128)(2,1)} %all-reduce.2.cloned.1.call-done, bf16[128,2048]{1,0:T(8,128)(2,1)S(1)} %copy-done.1), kind=kOutput, calls=%fused_computation.27 | convolution fusion | flops 269811712 | bytes 3277312 | tf_op jit(solution)/shard_map/dot_general | solution.py:61
  96.3 6.3 %all-gather.5.cloned.1.call-done = bf16[1024,1024]{0,1:T(8,128)(2,1)} async-done(((bf16[128,1024]{0,1:T(8,128)(2,1)}), bf16[1024,1024]{0,1:T(8,128)(2,1)}) %all-gather.5.cloned.1.call-update) | async-done | bytes 2097168 | tf_op jit(solution)/shard_map/all_gather | solution.py:66
  102.6 2.7 %fusion.51 = (bf16[1024,512]{0,1:T(8,128)(2,1)S(1)}, bf16[1024,512]{0,1:T(8,128)(2,1)}) fusion(bf16[1024,1024]{0,1:T(8,128)(2,1)} %all-gather.5.cloned.1.call-done), kind=kLoop, calls=%fused_computation.54 | loop fusion | bytes 4194304 | tf_op jit(solution)/shard_map/slice | solution.py:72
  105.3 2.1 %fusion.57 = (f32[4,128]{1,0:T(4,128)S(1)}, f32[4,128,1024]{2,1,0:T(8,128)}) fusion(bf16[1024,4,128]{0,2,1:T(8,128)(2,1)S(1)} %bitcast.62, bf16[16,4,8,128]{3,2,1,0:T(8,128)(2,1)S(1)} %fusion.23), kind=kOutput, calls=%fused_computation.56 | convolution fusion | flops 135791616 | bytes 3278848 | tf_op jit(solution)/shard_map/sub | solution.py:18
  107.5 2.6 %convolution_convert_fusion.5 = bf16[4,128,128]{2,1,0:T(8,128)(2,1)S(1)} fusion(bf16[1024,4,128]{0,2,1:T(8,128)(2,1)} %bitcast.63, f32[4,128,1024]{2,1,0:T(8,128)} %get-tuple-element.12, f32[4,128]{1,0:T(4,128)S(1)} %get-tuple-element.11), kind=kOutput, calls=%fused_computation.25 | convolution fusion | flops 135331840 | bytes 3278848 | tf_op jit(solution)/shard_map/hqk,khd->qhd/dot_general | solution.py:19
  110.0 1.3 convolution_convert_fusion
  111.3 21.8 %reduce-scatter.2.cloned.1.call-done = bf16[32,2048]{1,0:T(8,128)(2,1)} async-done(((bf16[128,2048]{1,0:T(8,128)(2,1)}), bf16[32,2048]{1,0:T(8,128)(2,1)}) %reduce-scatter.2.cloned.1.call-update) | async-done | bytes 131088 | tf_op jit(solution)/shard_map/reduce_scatter | solution.py:74
  133.1 1.7 %add_convert_fusion.1 = bf16[32,2048]{1,0:T(8,128)(2,1)} fusion(bf16[32,2048]{1,0:T(8,128)(2,1)} %reduce-scatter.2.cloned.1.call-done, f32[128,2048]{1,0:T(8,128)} %get-tuple-element.7, s32[]{:T(128)S(6)} %select_n.3), kind=kLoop, calls=%fused_computation.38 | loop fusion | flops 196608 | bytes 524292 | tf_op jit(solution)/shard_map/convert_element_type | solution.py:81
  (20 shorter events, 0.2 us)
Async XLA Ops:
  7.4 41.8 %copy-start = (bf16[512,2048]{1,0:T(8,128)(2,1)S(1)}, bf16[512,2048]{1,0:T(8,128)(2,1)}, u32[]{:S(2)}) copy-start(bf16[512,2048]{1,0:T(8,128)(2,1)} %param.20) | copy-start | bytes 6291460
  7.4 34.2 %copy-start.5 = (bf16[1024,512]{1,0:T(8,128)(2,1)S(1)}, bf16[1024,512]{1,0:T(8,128)(2,1)}, u32[]{:S(2)}) copy-start(bf16[1024,512]{1,0:T(8,128)(2,1)} %param.19) | copy-start | bytes 3145732
  7.4 34.2 %all-gather.3.cloned.1.call-start = ((), (), s32[]{:S(2)}) async-start(), calls=%async_computation.1 | async-start | bytes 1310720 | tf_op jit(solution)/shard_map/all_gather | solution.py:46
  10.8 81.5 %all-reduce.2.cloned.1.call-start = ((), (), s32[]{:S(2)}) async-start(), calls=%async_computation.2 | async-start | bytes 1048576 | tf_op jit(solution)/shard_map/psum | solution.py:55
  49.1 1.4 copy-start.4
  50.5 52.2 %all-gather.5.cloned.1.call-start = ((), (), s32[]{:S(2)}) async-start(), calls=%async_computation.3 | async-start | bytes 2359296 | tf_op jit(solution)/shard_map/all_gather | solution.py:66
  69.6 22.7 %copy-start.1 = (bf16[128,2048]{1,0:T(8,128)(2,1)S(1)}, bf16[128,2048]{1,0:T(8,128)(2,1)}, u32[]{:S(2)}) copy-start(bf16[128,2048]{1,0:T(8,128)(2,1)} %param.16) | copy-start | bytes 1572868
  73.9 59.2 %reduce-scatter.2.cloned.1.call-start = ((), (), s32[]{:S(2)}) async-start(), calls=%async_computation.4 | async-start | bytes 655360 | tf_op jit(solution)/shard_map/reduce_scatter | solution.py:74
  92.3 2.5 %copy-start.2 = (bf16[2048,512]{1,0:T(8,128)(2,1)S(1)}, bf16[2048,512]{1,0:T(8,128)(2,1)}, u32[]{:S(2)}) copy-start(bf16[2048,512]{1,0:T(8,128)(2,1)} %param.22) | copy-start | bytes 6291460
  107.5 2.6 %copy-start.3 = (bf16[512,2048]{1,0:T(8,128)(2,1)S(1)}, bf16[512,2048]{1,0:T(8,128)(2,1)}, u32[]{:S(2)}) copy-start(bf16[512,2048]{1,0:T(8,128)(2,1)} %param.25) | copy-start | bytes 6291460
Sparse Core Ops, SparseCore 0:
  10.9 30.6 all-gather.2
  50.6 41.6 all-reduce.1
  111.5 21.6 reduce-scatter.1
Sparse Core Ops, SparseCore 1:
  74.0 28.6 all-gather.4
where the time goes:
time: 142 us
  waiting for transfers between devices  75 us (53%)
  matrix products  23.4 us (16%)
  blocking collectives  19.1 us (13%)
  between operations  15.5 us (11%)
  other arithmetic  5.92 us (4%)
  local copies, waits for them, and re-layouts  3.01 us (2%)
    all_gather x1, waiting for transfers between devices, local(): lax.all_gather(keyed, 'inner', axis=0, tiled=True)  28.5 us
    reduce_scatter x1, waiting for transfers between devices, local(): lax.psum_scatter(jnp.dot(mixed_five, decode_output, preferred_element_typ...  21.8 us
    all_gather x1, blocking collectives, local(): outer_block = lax.all_gather(global_latents, 'inner', axis=0, tiled=True)  19.1 us
    psum x1, waiting for transfers between devices, local(): lax.psum(partial_value.astype(jnp.bfloat16), 'inner').astype(jnp.float32)  18.3 us
    all_gather x1, waiting for transfers between devices, local(): lax.all_gather(jnp.dot(outer_block, pair_five, preferred_element_type=jnp...  6.33 us
    dot_general x2, matrix products, attend(): jnp.einsum('hqk,khd->qhd', weights, values_in, preferred_element_type=jnp...  5.2 us
    dot_general x1, matrix products, local(): jnp.dot(outer_block, pair_five, preferred_element_type=jnp.float32)  4.32 us
  transfers between devices with their start and end apart: 4, of which 4 were waited for; matrix products, arithmetic and copies ran while one was open for 7% of the time, Pallas kernels for 0%

commit v1 on v0

v1 whole, which is shorter than its diff:
```python
import functools

import jax
import jax.numpy as jnp
from jax import lax
from jax.experimental import pallas as pl
from jax.experimental.pallas import tpu as pltpu
from jax.sharding import PartitionSpec as P

HEAD = 128
MESH = pl.DeviceIdType.MESH
F32 = jnp.float32
BF16 = jnp.bfloat16


def multiply(load, weight, store):
    columns = weight.shape[1]
    tile = min(256, columns)

    @pl.loop(0, columns // tile)
    def _(t):
        cols = pl.ds(pl.multiple_of(t * tile, tile), tile)
        store(cols, jnp.dot(load(), weight[:, cols], preferred_element_type=F32))


def flat(blocks):
    count, rows, columns = blocks.shape
    if rows % 16:
        return blocks.astype(F32).reshape(count * rows, columns).astype(BF16)
    return blocks.reshape(count * rows, columns)


def attend_head(query, keys, values):
    scores = lax.dot_general(
        query, keys, (((1,), (1,)), ((), ())), preferred_element_type=F32
    ) * (HEAD ** -0.5)
    top = jnp.max(scores, axis=-1, keepdims=True)
    raised = jnp.exp(scores - top)
    total = jnp.sum(raised, axis=-1, keepdims=True)
    mixed = jnp.dot(raised.astype(BF16), values, preferred_element_type=F32)
    return (mixed / total).astype(BF16)


class Chain:
    def __init__(self, buf, up, down, recv, me, count):
        self.buf, self.up, self.down, self.recv = buf, up, down, recv
        self.me, self.count = me, count

    def copy(self, block, sems, target):
        return pltpu.make_async_remote_copy(
            src_ref=self.buf.at[block],
            dst_ref=self.buf.at[block],
            send_sem=sems.at[block],
            recv_sem=self.recv.at[block],
            device_id={"inner": target},
            device_id_type=MESH,
        )

    def send_up(self, block):
        @pl.when(self.me < self.count - 1)
        def _():
            self.copy(block, self.up, self.me + 1).start()

    def send_down(self, block):
        @pl.when(self.me > 0)
        def _():
            self.copy(block, self.down, self.me - 1).start()

    def begin(self):
        self.send_up(self.me)
        self.send_down(self.me)

    def step(self, s, work=None):
        low, high = self.me - s, self.me + s

        @pl.when(low >= 0)
        def _():
            self.copy(low, self.up, self.me - 1).wait_recv()
            self.send_up(low)

        @pl.when(high < self.count)
        def _():
            self.copy(high, self.down, self.me + 1).wait_recv()
            self.send_down(high)

        if work is not None:

            @pl.when(low >= 0)
            def _():
                work(low)

            @pl.when(high < self.count)
            def _():
                work(high)

    def drain(self):
        for b in range(self.count):

            @pl.when((self.me >= b) & (self.me < self.count - 1))
            def _():
                self.copy(b, self.up, self.me + 1).wait_send()

            @pl.when((self.me <= b) & (self.me > 0))
            def _():
                self.copy(b, self.down, self.me - 1).wait_send()


class Scatter:
    def __init__(self, source, landing, send, recv, me, count):
        self.source, self.landing, self.send, self.recv = source, landing, send, recv
        self.me, self.count = me, count

    def copy(self, hop):
        target = lax.rem(self.me + hop, self.count)
        return pltpu.make_async_remote_copy(
            src_ref=self.source.at[target],
            dst_ref=self.landing.at[hop],
            send_sem=self.send.at[hop],
            recv_sem=self.recv.at[hop],
            device_id={"inner": target},
            device_id_type=MESH,
        )

    def begin(self):
        for hop in range(1, self.count):
            self.copy(hop).start()

    def total(self, own):
        total = own + self.source[self.me].astype(F32)
        for hop in range(1, self.count):
            self.copy(hop).wait_recv()
            total = total + self.landing[hop].astype(F32)
        return total

    def drain(self):
        for hop in range(1, self.count):
            self.copy(hop).wait_send()


def kernel(
    inner, outer,
    slot_in, group_in, embed_in, merge_in, qw_in, kw_in, vw_in, ow_in,
    global_in, dq_in, dk_in, dv_in, do_in,
    out_ref,
    embed, merge, group, qw, kw, vw, ow, dq, dk, dv, do,
    keyed, glob, key_two, value_two, query, mixed, merge_rows, level, pairs, normed,
    term_a, land_a, term_b, land_b,
    load_sem, k_up, k_down, k_recv, g_up, g_down, g_recv, n_up, n_down, n_recv,
    a_send, a_recv, b_send, b_recv, p_send, p_pass, p_recv,
):
    me = lax.axis_index("inner")
    place = lax.axis_index("outer")
    chips = outer // 2
    chip, core = place // 2, lax.rem(place, 2)
    width = qw.shape[1]
    heads = width // HEAD

    loads = [
        pltpu.make_async_copy(src, dst, load_sem.at[n])
        for n, (src, dst) in enumerate([
            (group_in, group), (embed_in, embed), (global_in, glob.at[me]), (merge_in, merge),
            (qw_in, qw), (kw_in, kw), (vw_in, vw), (ow_in, ow),
            (dk_in, dk), (dv_in, dv), (dq_in, dq), (do_in, do),
        ])
    ]
    for load in loads:
        load.start()

    barrier = pltpu.get_barrier_semaphore()
    for hop in range(1, inner):
        pl.semaphore_signal(
            barrier, inc=1, device_id={"inner": lax.rem(me + hop, inner)}, device_id_type=MESH
        )
    for hop in range(1, chips):
        pl.semaphore_signal(
            barrier, inc=1,
            device_id={"outer": lax.rem(chip + hop, chips) * 2 + core}, device_id_type=MESH,
        )
    partner = chip * 2 + 1 - core
    pl.semaphore_signal(barrier, inc=1, device_id={"outer": partner}, device_id_type=MESH)

    for n in (0, 1):
        loads[n].wait()
    slot = slot_in[0, 0]
    rows = lax.broadcasted_iota(jnp.int32, embed.shape, 0)
    vector = jnp.sum(
        jnp.where(rows == slot, embed[...].astype(F32), 0.0), axis=0, keepdims=True
    )
    keyed[me] = (group[...].astype(F32) + vector).astype(BF16)
    pl.semaphore_wait(barrier, inner - 1 + chips)

    chain_k = Chain(keyed, k_up, k_down, k_recv, me, inner)
    chain_g = Chain(glob, g_up, g_down, g_recv, me, inner)
    chain_n = Chain(normed, n_up, n_down, n_recv, me, inner)
    sum_a = Scatter(term_a, land_a, a_send, a_recv, me, inner)
    sum_b = Scatter(term_b, land_b, b_send, b_recv, me, inner)

    chain_k.begin()

    for n in (2, 3, 4):
        loads[n].wait()
    merge_rows[...] = merge[...].astype(F32).reshape(merge_rows.shape)

    def put_query(cols, value):
        query[:, cols] = value.astype(BF16)

    multiply(lambda: merge[...], qw, put_query)

    for n in (5, 6):
        loads[n].wait()

    def keys_values(block):
        def put_key(cols, value):
            key_two[block, :, cols] = value.astype(BF16)

        def put_value(cols, value):
            value_two[block, :, cols] = value.astype(BF16)

        multiply(lambda: keyed[block], kw, put_key)
        multiply(lambda: keyed[block], vw, put_value)

    keys_values(me)
    for s in range(1, inner):
        if s == inner - 1:
            chain_k.step(s)
            chain_g.begin()

            @pl.when(me - s >= 0)
            def _():
                keys_values(me - s)

            @pl.when(me + s < inner)
            def _():
                keys_values(me + s)
        else:
            chain_k.step(s, keys_values)

    steps = list(range(1, inner))
    for h in range(heads):
        cols = slice(h * HEAD, (h + 1) * HEAD)
        mixed[:, cols] = attend_head(
            query[:, cols], flat(key_two[:, :, cols]), flat(value_two[:, :, cols])
        )
        if h % 2 and steps:
            chain_g.step(steps.pop(0))

    loads[7].wait()

    def put_term(term):
        def put(cols, value):
            term[:, :, cols] = value.reshape(
                inner, term.shape[1], value.shape[1]
            ).astype(BF16)

        return put

    multiply(lambda: mixed[...], ow, put_term(term_a))
    sum_a.begin()

    for s in steps:
        chain_g.step(s)
    for n in (8, 9):
        loads[n].wait()

    def put_pair(start):
        def put(cols, value):
            shifted = pl.ds(pl.multiple_of(cols.start + start, HEAD), cols.size)
            pairs[place, :, shifted] = value.astype(BF16)

        return put

    multiply(lambda: flat(glob[...]), dk, put_pair(0))
    multiply(lambda: flat(glob[...]), dv, put_pair(width))

    def direct(hop):
        target = lax.rem(chip + hop, chips) * 2 + core
        return pltpu.make_async_remote_copy(
            src_ref=pairs.at[place], dst_ref=pairs.at[place],
            send_sem=p_send.at[hop], recv_sem=p_recv.at[place],
            device_id={"outer": target}, device_id_type=MESH,
        )

    def arrival(block):
        return pltpu.make_async_remote_copy(
            src_ref=pairs.at[block], dst_ref=pairs.at[block],
            send_sem=p_pass.at[0], recv_sem=p_recv.at[block],
            device_id={"outer": partner}, device_id_type=MESH,
        )

    def onward(hop):
        block = lax.rem(chip + hop, chips) * 2 + core
        return pltpu.make_async_remote_copy(
            src_ref=pairs.at[block], dst_ref=pairs.at[block],
            send_sem=p_pass.at[hop], recv_sem=p_recv.at[block],
            device_id={"outer": partner}, device_id_type=MESH,
        )

    for hop in range(1, chips):
        direct(hop).start()
    onward(0).start()

    own = sum_a.total(merge_rows[me])
    level[...] = own
    scale = lax.rsqrt(jnp.mean(own * own, axis=-1, keepdims=True) + 1e-6)
    normed[me] = (own * scale).astype(BF16)
    chain_n.begin()
    for s in range(1, inner):
        chain_n.step(s)
    loads[10].wait()
    multiply(lambda: flat(normed[...]), dq, put_query)

    for hop in range(1, chips):
        arrival(lax.rem(chip + hop, chips) * 2 + core).wait_recv()
        onward(hop).start()
    for hop in range(chips):
        arrival(lax.rem(chip + hop, chips) * 2 + 1 - core).wait_recv()

    for h in range(heads):
        cols = slice(h * HEAD, (h + 1) * HEAD)
        after = slice(width + h * HEAD, width + (h + 1) * HEAD)
        mixed[:, cols] = attend_head(
            query[:, cols], flat(pairs[:, :, cols]), flat(pairs[:, :, after])
        )
    loads[11].wait()
    multiply(lambda: mixed[...], do, put_term(term_b))
    sum_b.begin()

    chain_k.drain()
    chain_g.drain()
    chain_n.drain()
    sum_a.drain()
    for hop in range(1, chips):
        direct(hop).wait_send()
    for hop in range(chips):
        onward(hop).wait_send()
    out_ref[...] = sum_b.total(level[...]).astype(BF16)
    sum_b.drain()


def local(inner, outer, group, slot_ids, embed, merge, qw, kw, vw, ow, glob, dq, dk, dv, do):
    rows, depth = group.shape
    queries, wide = merge.shape
    width = qw.shape[1]
    own = queries // inner
    blocks = glob.shape[0] * inner
    dma = pltpu.SemaphoreType.DMA
    vmem = lambda *shape, kind=BF16: pltpu.VMEM(shape, kind)
    same = lambda array: pltpu.VMEM(array.shape, array.dtype)
    scratch = [
        same(embed), same(merge), same(group), same(qw), same(kw), same(vw), same(ow),
        same(dq), same(dk), same(dv), same(do),
        vmem(inner, rows, depth),
        vmem(inner, glob.shape[0], wide),
        vmem(inner, rows, width),
        vmem(inner, rows, width),
        vmem(queries, width),
        vmem(queries, width),
        vmem(inner, own, wide, kind=F32),
        vmem(own, wide, kind=F32),
        vmem(outer, blocks, 2 * width),
        vmem(inner, own, wide),
        vmem(inner, own, wide), vmem(inner, own, wide),
        vmem(inner, own, wide), vmem(inner, own, wide),
        dma((12,)),
    ] + [dma((inner,))] * 13 + [dma((outer // 2,))] * 2 + [dma((outer,))]
    any_space = pl.BlockSpec(memory_space=pl.ANY)
    return pl.pallas_call(
        functools.partial(kernel, inner, outer),
        out_shape=jax.ShapeDtypeStruct((own, wide), BF16),
        in_specs=[pl.BlockSpec(memory_space=pltpu.SMEM)] + [any_space] * 12,
        out_specs=pl.BlockSpec(memory_space=pltpu.VMEM),
        scratch_shapes=scratch,
        compiler_params=pltpu.CompilerParams(
            collective_id=0, has_side_effects=True, vmem_limit_bytes=56 * 2 ** 20
        ),
    )(slot_ids, group, embed, merge, qw, kw, vw, ow, glob, dq, dk, dv, do)


def solution(mesh):
    rows = P(("outer", "inner"), None)
    split = P(None, "inner")
    down = P("inner", None)
    return jax.shard_map(
        functools.partial(local, mesh.shape["inner"], mesh.shape["outer"]),
        mesh=mesh,
        in_specs=(
            rows, P("outer", "inner"), P(), P(), split, split, split, down,
            rows, split, split, split, down,
        ),
        out_specs=rows,
        check_vma=False,
    )
```

time: 142 us -> 81 us (0.57)
  Pallas kernels: 0 us -> 77.3 us
  waiting for transfers between devices: 75 us -> 0 us
  matrix products: 23.4 us -> 0 us
  blocking collectives: 19.1 us -> 0 us
  between operations: 15.5 us -> 0.66 us
  other arithmetic: 5.92 us -> 0 us
  local copies, waits for them, and re-layouts: 3.01 us -> 1.57 us
    pallas_call x0 -> x1, Pallas kernels: none -> 77.3 us  [local(): pl.pallas_call(functools.partial(kernel, inner, outer), out_shape=jax.Sha...]
    all_gather x2 -> x0, waiting for transfers between devices: 34.8 us -> none  [the longest x1 28.5 us: local(): lax.all_gather(keyed, 'inner', axis=0, tiled=True)]
    reduce_scatter x1 -> x0, waiting for transfers between devices: 21.8 us -> none  [local(): lax.psum_scatter(jnp.dot(mixed_five, decode_output, preferred_element_typ...]
    dot_general x10 -> x0, matrix products: 20.8 us -> none  [the longest x2 5.2 us: attend(): jnp.einsum('hqk,khd->qhd', weights, values_in, preferred_element_type=jnp...]
    all_gather x1 -> x0, blocking collectives: 19.1 us -> none  [local(): outer_block = lax.all_gather(global_latents, 'inner', axis=0, tiled=True)]
    psum x1 -> x0, waiting for transfers between devices: 18.3 us -> none  [local(): lax.psum(partial_value.astype(jnp.bfloat16), 'inner').astype(jnp.float32)]
    convert_element_type x2 -> x0, other arithmetic: 3.42 us -> none  [the longest x1 1.72 us: local(): (group_latents.astype(jnp.float32) + slot_vector).astype(jnp.bfloat16)]
    slice x1 -> x0, local copies, waits for them, and re-layouts: 2.69 us -> none  [local(): global_pairs[:, :columns]]
  transfers between devices with their start and end apart: 4 -> 0, of which waited for: 4 -> 0; matrix products, arithmetic and copies ran while one was open for 7% -> 0% of each run, Pallas kernels for 0% -> 0%
where the time goes in v1:
time: 81 us; the launch traced here: 79.6 us
  Pallas kernels  77.3 us (95%)
  local copies, waits for them, and re-layouts  1.57 us (2%)
    pallas_call x1, Pallas kernels, local(): pl.pallas_call(functools.partial(kernel, inner, outer), out_shape=jax.Sha...  77.3 us

profile of v1, /device:TPU:0, one launch (start us, length us, event | category | flops | bytes accessed | tf_op | source)
XLA Modules:
  0.0 79.6 jit_solution(6924835895772765352)
XLA Ops:
  0.7 77.3 %shard_map.127 = bf16[32,2048]{1,0:T(8,128)(2,1)} custom-call(s32[1,1]{1,0:T(1,128)S(6)} %copy.15.slot_in, bf16[128,1024]{1,0:T(8,128)(2,1)} %group_in.1, bf16[4,1024]{1,0:T(4,128)(2,1)} %embed_in.1, bf16[128,2048]{1,0:T(8,128)(2,1)} %merge_in.1, bf16[2048,512]{1,0:T(8,128)(2,1)} %qw_in.1, bf16[1024,512]{1,0:T(8,128)(2,1)} %kw_in.1, ...), custom_call_target="tpu_custom_call" | custom-call | tf_op jit(solution)/shard_map/pallas_call | solution.py:367
  78.0 1.6 %copy.16 = bf16[32,2048]{1,0:T(8,128)(2,1)} copy(bf16[32,2048]{1,0:T(8,128)(2,1)} %shard_map.127) | data formatting | bytes 262144

commit v2 on v1

--- a/solution.py
+++ b/solution.py
@@ -41,48 +41,57 @@
     return (mixed / total).astype(BF16)
 
 
-class Chain:
+class Spread:
     def __init__(self, buf, up, down, recv, me, count):
         self.buf, self.up, self.down, self.recv = buf, up, down, recv
         self.me, self.count = me, count
 
-    def copy(self, block, sems, target):
+    def copy(self, block, sem, target):
         return pltpu.make_async_remote_copy(
             src_ref=self.buf.at[block],
             dst_ref=self.buf.at[block],
-            send_sem=sems.at[block],
+            send_sem=sem,
             recv_sem=self.recv.at[block],
             device_id={"inner": target},
             device_id_type=MESH,
         )
 
-    def send_up(self, block):
-        @pl.when(self.me < self.count - 1)
-        def _():
-            self.copy(block, self.up, self.me + 1).start()
-
-    def send_down(self, block):
-        @pl.when(self.me > 0)
-        def _():
-            self.copy(block, self.down, self.me - 1).start()
+    def own(self, act):
+        for hop in range(self.count - 1, 0, -1):
+            last = 1 if hop == 1 else 2
+
+            @pl.when(self.me + hop <= self.count - last)
+            def _():
+                act(self.copy(self.me, self.up.at[hop, 0], self.me + hop))
+
+            @pl.when(self.me - hop >= last - 1)
+            def _():
+                act(self.copy(self.me, self.down.at[hop, 0], self.me - hop))
 
     def begin(self):
-        self.send_up(self.me)
-        self.send_down(self.me)
+        self.own(lambda copy: copy.start())
+
+    def onward(self, s, act):
+        @pl.when((self.me == self.count - 2) & (self.me - s >= 0))
+        def _():
+            act(self.copy(self.me - s, self.up.at[s, 1], self.count - 1))
+
+        @pl.when((self.me == 1) & (self.me + s < self.count))
+        def _():
+            act(self.copy(self.me + s, self.down.at[s, 1], 0))
 
     def step(self, s, work=None):
         low, high = self.me - s, self.me + s
 
         @pl.when(low >= 0)
         def _():
-            self.copy(low, self.up, self.me - 1).wait_recv()
-            self.send_up(low)
+            self.copy(low, self.up.at[s, 1], self.me - 1).wait_recv()
 
         @pl.when(high < self.count)
         def _():
-            self.copy(high, self.down, self.me + 1).wait_recv()
-            self.send_down(high)
-
+            self.copy(high, self.down.at[s, 1], self.me + 1).wait_recv()
+
+        self.onward(s, lambda copy: copy.start())
         if work is not None:
 
             @pl.when(low >= 0)
@@ -94,47 +103,117 @@
                 work(high)
 
     def drain(self):
-        for b in range(self.count):
-
-            @pl.when((self.me >= b) & (self.me < self.count - 1))
-            def _():
-                self.copy(b, self.up, self.me + 1).wait_send()
-
-            @pl.when((self.me <= b) & (self.me > 0))
-            def _():
-                self.copy(b, self.down, self.me - 1).wait_send()
+        self.own(lambda copy: copy.wait_send())
+        for s in range(1, self.count):
+            self.onward(s, lambda copy: copy.wait_send())
 
 
 class Scatter:
-    def __init__(self, source, landing, send, recv, me, count):
-        self.source, self.landing, self.send, self.recv = source, landing, send, recv
+    def __init__(self, term, relay, landing, send, recv, passed, me, count):
+        self.term, self.relay, self.landing = term, relay, landing
+        self.send, self.recv, self.passed = send, recv, passed
         self.me, self.count = me, count
 
-    def copy(self, hop):
-        target = lax.rem(self.me + hop, self.count)
-        return pltpu.make_async_remote_copy(
-            src_ref=self.source.at[target],
-            dst_ref=self.landing.at[hop],
-            send_sem=self.send.at[hop],
-            recv_sem=self.recv.at[hop],
+    def to(self, block, target):
+        return pltpu.make_async_remote_copy(
+            src_ref=self.term.at[block],
+            dst_ref=self.landing.at[self.me],
+            send_sem=self.send.at[block],
+            recv_sem=self.recv.at[self.me],
             device_id={"inner": target},
             device_id_type=MESH,
         )
 
-    def begin(self):
-        for hop in range(1, self.count):
-            self.copy(hop).start()
-
-    def total(self, own):
-        total = own + self.source[self.me].astype(F32)
-        for hop in range(1, self.count):
-            self.copy(hop).wait_recv()
-            total = total + self.landing[hop].astype(F32)
-        return total
+    def via(self, block, target):
+        return pltpu.make_async_remote_copy(
+            src_ref=self.term.at[block],
+            dst_ref=self.relay.at[block],
+            send_sem=self.send.at[block],
+            recv_sem=self.passed.at[block],
+            device_id={"inner": target},
+            device_id_type=MESH,
+        )
+
+    def came(self, source):
+        pltpu.make_async_remote_copy(
+            src_ref=self.landing.at[source],
+            dst_ref=self.landing.at[source],
+            send_sem=self.send.at[source],
+            recv_sem=self.recv.at[source],
+            device_id={"inner": source},
+            device_id_type=MESH,
+        ).wait_recv()
+
+    def add(self, block, end):
+        self.via(block, end).wait_recv()
+        self.term[block] = (
+            self.term[block].astype(F32) + self.relay[block].astype(F32)
+        ).astype(BF16)
+        self.to(block, block).start()
+
+    def run(self):
+        count, me = self.count, self.me
+
+        @pl.when(me == 0)
+        def _():
+            for block in range(count - 1, 1, -1):
+                self.via(block, 1).start()
+            self.to(1, 1).start()
+
+        @pl.when(me == count - 1)
+        def _():
+            for block in range(count - 2):
+                self.via(block, count - 2).start()
+            self.to(count - 2, count - 2).start()
+
+        for far in range(count):
+
+            @pl.when((me > 0) & (me < count - 2) & (count - 1 - far > me) & (me > 1))
+            def _():
+                self.to(count - 1 - far, count - 1 - far).start()
+
+            @pl.when((me == count - 2) & (count - 1 - far > me))
+            def _():
+                self.to(count - 1 - far, count - 1 - far).start()
+
+            @pl.when((me > 1) & (me < count - 2) & (far < me))
+            def _():
+                self.to(far, far).start()
+
+            @pl.when((me == 1) & (far < me))
+            def _():
+                self.to(far, far).start()
+
+        @pl.when(me == 1)
+        def _():
+            for block in range(count - 1, 1, -1):
+                self.add(block, 0)
+
+        @pl.when(me == count - 2)
+        def _():
+            for block in range(count - 2):
+                self.add(block, count - 1)
+
+    def total(self, own, into):
+        into[...] = own + self.term[self.me].astype(F32)
+        for source in range(self.count):
+            there = self.me != source
+            if source == 0:
+                there = self.me == 1
+            if source == self.count - 1:
+                there = self.me == self.count - 2
+
+            @pl.when(there)
+            def _():
+                self.came(source)
+                into[...] += self.landing[source].astype(F32)
 
     def drain(self):
-        for hop in range(1, self.count):
-            self.copy(hop).wait_send()
+        for block in range(self.count):
+
+            @pl.when(self.me != block)
+            def _():
+                self.to(block, block).wait_send()
 
 
 def kernel(
@@ -144,9 +223,9 @@
     out_ref,
     embed, merge, group, qw, kw, vw, ow, dq, dk, dv, do,
     keyed, glob, key_two, value_two, query, mixed, merge_rows, level, pairs, normed,
-    term_a, land_a, term_b, land_b,
+    term_a, relay_a, land_a, term_b, relay_b, land_b,
     load_sem, k_up, k_down, k_recv, g_up, g_down, g_recv, n_up, n_down, n_recv,
-    a_send, a_recv, b_send, b_recv, p_send, p_pass, p_recv,
+    a_send, a_recv, a_pass, b_send, b_recv, b_pass, p_send, p_pass, p_recv,
 ):
     me = lax.axis_index("inner")
     place = lax.axis_index("outer")
@@ -189,11 +268,11 @@
     keyed[me] = (group[...].astype(F32) + vector).astype(BF16)
     pl.semaphore_wait(barrier, inner - 1 + chips)
 
-    chain_k = Chain(keyed, k_up, k_down, k_recv, me, inner)
-    chain_g = Chain(glob, g_up, g_down, g_recv, me, inner)
-    chain_n = Chain(normed, n_up, n_down, n_recv, me, inner)
-    sum_a = Scatter(term_a, land_a, a_send, a_recv, me, inner)
-    sum_b = Scatter(term_b, land_b, b_send, b_recv, me, inner)
+    chain_k = Spread(keyed, k_up, k_down, k_recv, me, inner)
+    chain_g = Spread(glob, g_up, g_down, g_recv, me, inner)
+    chain_n = Spread(normed, n_up, n_down, n_recv, me, inner)
+    sum_a = Scatter(term_a, relay_a, land_a, a_send, a_recv, a_pass, me, inner)
+    sum_b = Scatter(term_b, relay_b, land_b, b_send, b_recv, b_pass, me, inner)
 
     chain_k.begin()
 
@@ -219,11 +298,11 @@
         multiply(lambda: keyed[block], kw, put_key)
         multiply(lambda: keyed[block], vw, put_value)
 
+    chain_g.begin()
     keys_values(me)
     for s in range(1, inner):
         if s == inner - 1:
             chain_k.step(s)
-            chain_g.begin()
 
             @pl.when(me - s >= 0)
             def _():
@@ -255,7 +334,7 @@
         return put
 
     multiply(lambda: mixed[...], ow, put_term(term_a))
-    sum_a.begin()
+    sum_a.run()
 
     for s in steps:
         chain_g.step(s)
@@ -299,19 +378,19 @@
         direct(hop).start()
     onward(0).start()
 
-    own = sum_a.total(merge_rows[me])
-    level[...] = own
+    sum_a.total(merge_rows[me], level)
+    own = level[...]
     scale = lax.rsqrt(jnp.mean(own * own, axis=-1, keepdims=True) + 1e-6)
     normed[me] = (own * scale).astype(BF16)
     chain_n.begin()
+    for hop in range(1, chips):
+        arrival(lax.rem(chip + hop, chips) * 2 + core).wait_recv()
+        onward(hop).start()
     for s in range(1, inner):
         chain_n.step(s)
     loads[10].wait()
     multiply(lambda: flat(normed[...]), dq, put_query)
 
-    for hop in range(1, chips):
-        arrival(lax.rem(chip + hop, chips) * 2 + core).wait_recv()
-        onward(hop).start()
     for hop in range(chips):
         arrival(lax.rem(chip + hop, chips) * 2 + 1 - core).wait_recv()
 
@@ -323,7 +402,7 @@
         )
     loads[11].wait()
     multiply(lambda: mixed[...], do, put_term(term_b))
-    sum_b.begin()
+    sum_b.run()
 
     chain_k.drain()
     chain_g.drain()
@@ -333,7 +412,8 @@
         direct(hop).wait_send()
     for hop in range(chips):
         onward(hop).wait_send()
-    out_ref[...] = sum_b.total(level[...]).astype(BF16)
+    sum_b.total(level[...], level)
+    out_ref[...] = level[...].astype(BF16)
     sum_b.drain()
 
 
@@ -359,10 +439,9 @@
         vmem(own, wide, kind=F32),
         vmem(outer, blocks, 2 * width),
         vmem(inner, own, wide),
-        vmem(inner, own, wide), vmem(inner, own, wide),
-        vmem(inner, own, wide), vmem(inner, own, wide),
+    ] + [vmem(inner, own, wide)] * 6 + [
         dma((12,)),
-    ] + [dma((inner,))] * 13 + [dma((outer // 2,))] * 2 + [dma((outer,))]
+    ] + [dma((inner, 2)), dma((inner, 2)), dma((inner,))] * 3 + [dma((inner,))] * 6 + [dma((outer // 2,))] * 2 + [dma((outer,))]
     any_space = pl.BlockSpec(memory_space=pl.ANY)
     return pl.pallas_call(
         functools.partial(kernel, inner, outer),

time: 81 us -> 76.9 us (0.949); the launches traced: 79.6 us -> 76.8 us
  Pallas kernels: 77.3 us -> 74.5 us
    pallas_call x1, Pallas kernels: 77.3 us -> 74.5 us  [local(): pl.pallas_call(functools.partial(kernel, inner, outer), out_shape=jax.Sha...]
where the time goes in v2:
time: 76.9 us; the launch traced here: 76.8 us
  Pallas kernels  74.5 us (97%)
  local copies, waits for them, and re-layouts  1.57 us (2%)
    pallas_call x1, Pallas kernels, local(): pl.pallas_call(functools.partial(kernel, inner, outer), out_shape=jax.Sha...  74.5 us
    unnamed x1, local copies, waits for them, and re-layouts  1.57 us

profile of v2, /device:TPU:0, one launch (start us, length us, event | category | flops | bytes accessed | tf_op | source)
XLA Modules:
  0.0 76.8 jit_solution(16999084192803427786)
XLA Ops:
  0.7 74.5 %shard_map.127 = bf16[32,2048]{1,0:T(8,128)(2,1)} custom-call(s32[1,1]{1,0:T(1,128)S(6)} %copy.15.slot_in, bf16[128,1024]{1,0:T(8,128)(2,1)} %group_in.1, bf16[4,1024]{1,0:T(4,128)(2,1)} %embed_in.1, bf16[128,2048]{1,0:T(8,128)(2,1)} %merge_in.1, bf16[2048,512]{1,0:T(8,128)(2,1)} %qw_in.1, bf16[1024,512]{1,0:T(8,128)(2,1)} %kw_in.1, ...), custom_call_target="tpu_custom_call" | custom-call | tf_op jit(solution)/shard_map/pallas_call | solution.py:446
  75.2 1.6 %copy.16 = bf16[32,2048]{1,0:T(8,128)(2,1)} copy(bf16[32,2048]{1,0:T(8,128)(2,1)} %shard_map.127) | data formatting | bytes 262144

commit v3 on v2

--- a/solution.py
+++ b/solution.py
@@ -15,7 +15,7 @@
 
 def multiply(load, weight, store):
     columns = weight.shape[1]
-    tile = min(256, columns)
+    tile = min(512, columns)
 
     @pl.loop(0, columns // tile)
     def _(t):
@@ -320,7 +320,7 @@
         mixed[:, cols] = attend_head(
             query[:, cols], flat(key_two[:, :, cols]), flat(value_two[:, :, cols])
         )
-        if h % 2 and steps:
+        if steps:
             chain_g.step(steps.pop(0))
 
     loads[7].wait()

time: 76.9 us -> 75.7 us (0.984)
  Pallas kernels: 74.5 us -> 73.3 us
    pallas_call x1, Pallas kernels: 74.5 us -> 73.3 us  [local(): pl.pallas_call(functools.partial(kernel, inner, outer), out_shape=jax.Sha...]
where the time goes in v3:
time: 75.7 us; the launch traced here: 75.6 us
  Pallas kernels  73.3 us (97%)
  local copies, waits for them, and re-layouts  1.57 us (2%)
    pallas_call x1, Pallas kernels, local(): pl.pallas_call(functools.partial(kernel, inner, outer), out_shape=jax.Sha...  73.3 us
    unnamed x1, local copies, waits for them, and re-layouts  1.57 us

profile of v3, /device:TPU:0, one launch (start us, length us, event | category | flops | bytes accessed | tf_op | source)
XLA Modules:
  0.0 75.6 jit_solution(7966519740969872971)
XLA Ops:
  0.7 73.3 %shard_map.127 = bf16[32,2048]{1,0:T(8,128)(2,1)} custom-call(s32[1,1]{1,0:T(1,128)S(6)} %copy.15.slot_in, bf16[128,1024]{1,0:T(8,128)(2,1)} %group_in.1, bf16[4,1024]{1,0:T(4,128)(2,1)} %embed_in.1, bf16[128,2048]{1,0:T(8,128)(2,1)} %merge_in.1, bf16[2048,512]{1,0:T(8,128)(2,1)} %qw_in.1, bf16[1024,512]{1,0:T(8,128)(2,1)} %kw_in.1, ...), custom_call_target="tpu_custom_call" | custom-call | tf_op jit(solution)/shard_map/pallas_call | solution.py:446
  74.0 1.6 %copy.16 = bf16[32,2048]{1,0:T(8,128)(2,1)} copy(bf16[32,2048]{1,0:T(8,128)(2,1)} %shard_map.127) | data formatting | bytes 262144
